TPU v7x, 32 devices: a whole 2x2x4 slice. The times are simulated.
32 devices in a mesh: row: 4 (over z), col: 4 (over x, core), dp: 2 (over y).
Axes of the slice: x: 2, y: 2, z: 4, core: 2. Of those that a mesh axis runs over, the one named last changes fastest.
Arguments:
- hidden_states: bfloat16 [2048, 1536], P(('dp', 'row'), 'col'), may hold values from -18 to 18
- w_query: bfloat16 [1536, 1536], P('col', 'row'), may hold values from -0.102062073 to 0.102062073
- w_key_value: bfloat16 [1536, 512], P('col'), may hold values from -0.102062073 to 0.102062073
- adapter_down: bfloat16 [128, 1536, 16], P('dp', 'col'), may hold values from -0.15625 to 0.15625
- adapter_up: bfloat16 [128, 16, 1536], P('dp', None, 'row'), may hold values from -1.5 to 1.5
- req_lengths: int32 [2, 8], replicated, may hold values from 1 to 160, 960 in all within a row
- req_adapter: int32 [2, 8], replicated, may hold values from 0 to 127, as said below
Outputs:
- attention: bfloat16 [2048, 1536], P(('dp', 'col'), 'row')
- kv_cache: bfloat16 [2048, 512], P(('dp', 'col'))
Inputs may be any that keep to these rules, and one draw needn't show every extreme that they name: `req_lengths`: the lengths of one block sum to 960, and each block has a request of exactly 160 tokens. `req_adapter`: adapters k * 64 to (k + 1) * 64 - 1 are those of index k of dp; the requests of one block use adapters of one index of dp at most 4 times, and some index of dp is used exactly that often by every block.
All inputs are finite; a program needn't handle non-finite values.
Results may differ from a plain program's by a relative error of at most 0.0072.
Values may be sent and summed in bfloat16 or wider, within the bound.
A program may use at most 128 MiB of HBM per device.

v0:
```python
import math

import jax
import jax.numpy as jnp
from jax import lax
from jax.sharding import PartitionSpec as P

HEAD_DIM = 128
MOST_LEN = 160


masked_score = -1e30


def block_layout(lengths_row, block_len):
    prefix_len = block_len - jnp.sum(lengths_row)
    ends_at = jnp.cumsum(lengths_row) + prefix_len
    starts = ends_at - lengths_row
    positions = jnp.arange(block_len, dtype=jnp.int32)
    segment = jnp.sum((positions[:, None] >= starts[None, :]).astype(jnp.int32), axis=1)
    return (starts, segment, positions)


def slot_numbers(holders):
    request_total = holders.shape[0]
    ordering = jnp.arange(request_total, dtype=jnp.int32)
    earlier = ordering[None, :] < ordering[:, None]
    same_holder = holders[:, None] == holders[None, :]
    return jnp.sum((earlier & same_holder).astype(jnp.int32), axis=1)


def make_attend(query_rows, segment, first_row, kv_group, head_size, kv_half):
    own_rows = query_rows.shape[0]
    heads_here = query_rows.shape[1] // head_size
    query_heads = query_rows.reshape(own_rows, heads_here, head_size)
    query_pos = first_row + jnp.arange(own_rows, dtype=jnp.int32)
    query_seg = lax.dynamic_slice_in_dim(segment, first_row, own_rows, 0)
    score_scale = 1.0 / math.sqrt(head_size)

    def attend(state_in, key_block, key_start):
        running_max, running_sum, running_out = state_in
        block_size = key_block.shape[0]
        key_rows = lax.dynamic_slice_in_dim(key_block, kv_group * head_size, head_size, 1)
        values = lax.dynamic_slice_in_dim(key_block, kv_half + kv_group * head_size, head_size, 1)
        key_pos = jnp.arange(block_size, dtype=jnp.int32)
        allowed = (key_pos[None, :] <= query_pos[:, None]) & (
            (segment[None, :] == query_seg[:, None]) | (segment[None, :] == 0)
        )
        scores = (
            jnp.einsum("qhd,kd->hqk", query_heads, key_rows, preferred_element_type=jnp.float32)
            * score_scale
        )
        scores = jnp.where(allowed[None], scores, masked_score)
        new_max = jnp.maximum(running_max, jnp.max(scores, axis=2))
        weights = jnp.where(allowed[None], jnp.exp(scores - new_max[:, :, None]), 0.0)
        running_sum = jnp.sum(weights, axis=2)
        running_out = jnp.einsum(
            "hqk,kd->hqd", weights.astype(jnp.bfloat16), values, preferred_element_type=jnp.float32
        )
        return (new_max, running_sum, running_out)

    initial = (
        jnp.full((heads_here, own_rows), masked_score, jnp.float32),
        jnp.zeros((heads_here, own_rows), jnp.float32),
        jnp.zeros((heads_here, own_rows, head_size), jnp.float32),
    )
    return (attend, initial)


def body(hidden_states, w_query, w_key_value, adapter_down, adapter_up, req_lengths, req_adapter):
    dp_size = lax.axis_size("dp")
    block_index = lax.axis_index("dp")
    col_index = lax.axis_index("col")
    row_index = lax.axis_index("row")
    gathered = lax.all_gather(hidden_states, "row", axis=0, tiled=True)
    block_len = gathered.shape[0]
    query_cols = w_query.shape[1]
    kv_cols = w_key_value.shape[1]
    kv_half = kv_cols // 2
    head_size = HEAD_DIM
    heads_here = query_cols // head_size
    heads_total = heads_here * lax.axis_size("row")
    kv_heads = kv_half // head_size
    kv_group = row_index * heads_here // (heads_total // kv_heads)
    own_rows = block_len // lax.axis_size("col")
    first_row = col_index * own_rows
    held_sets = adapter_down.shape[0]
    width_here = adapter_down.shape[1]
    rank_size = adapter_down.shape[2]
    lengths_row = req_lengths[block_index]
    adapters_row = req_adapter[block_index]
    requests = lengths_row.shape[0]
    starts, segment, positions = block_layout(lengths_row, block_len)
    request_of = jnp.clip(segment - 1, 0, requests - 1)
    in_request = segment > 0
    holders = adapters_row // held_sets
    slot_of = slot_numbers(holders)
    per_holder = (requests + dp_size - 1) // dp_size
    longest = MOST_LEN
    target_ids = jnp.arange(dp_size, dtype=jnp.int32)[:, None, None]
    slot_ids = jnp.arange(per_holder, dtype=jnp.int32)[None, :, None]
    pairing = (holders[None, None, :] == target_ids) & (slot_of[None, None, :] == slot_ids)
    pair_int = pairing.astype(jnp.int32)
    slot_start = jnp.sum(pair_int * starts[None, None, :], axis=2)
    slot_len = jnp.sum(pair_int * lengths_row[None, None, :], axis=2)
    slot_adapter = jnp.where(
        jnp.any(pairing, axis=2),
        jnp.sum(pair_int * (adapters_row % held_sets)[None, None, :], axis=2),
        -1,
    )
    offsets = jnp.arange(longest, dtype=jnp.int32)
    token_at = slot_start[:, :, None] + offsets[None, None, :]
    live_rows = offsets[None, None, :] < slot_len[:, :, None]
    outgoing = jnp.where(
        live_rows[..., None],
        gathered[jnp.clip(token_at, 0, block_len - 1)],
        jnp.zeros((), gathered.dtype),
    )
    flat_down = jnp.transpose(adapter_down, (1, 0, 2)).reshape(width_here, held_sets * rank_size)
    flat_up = adapter_up.reshape(held_sets * rank_size, query_cols).astype(jnp.float32)
    rank_owner = jnp.arange(held_sets * rank_size, dtype=jnp.int32) // rank_size
    sent_rows = lax.all_to_all(outgoing, "dp", split_axis=0, concat_axis=0, tiled=True)
    sent_ids = lax.all_to_all(
        slot_adapter.astype(jnp.bfloat16), "dp", split_axis=0, concat_axis=0, tiled=True
    )
    reduced = jnp.einsum("nkld,da->nkla", sent_rows, flat_down, preferred_element_type=jnp.float32)
    kept_cols = rank_owner[None, None, :] == sent_ids.astype(jnp.int32)[:, :, None]
    reduced = jnp.where(kept_cols[:, :, None, :], reduced, 0.0)
    adapter_part = jnp.einsum("nkla,af->nklf", reduced, flat_up, precision=lax.Precision.HIGHEST)
    returned = lax.all_to_all(adapter_part, "dp", split_axis=0, concat_axis=0, tiled=True)
    flat_index = (holders[request_of] * per_holder + slot_of[request_of]) * longest + jnp.clip(
        positions - starts[request_of], 0, longest - 1
    )
    adapter_term = returned.reshape(-1, query_cols)[flat_index]
    adapter_term = jnp.where(in_request[:, None], adapter_term, 0.0)
    both_weights = jnp.concatenate([w_query, w_key_value], axis=1)
    partial_value = jnp.dot(gathered, both_weights, preferred_element_type=jnp.float32)
    summed = lax.psum_scatter(
        partial_value
        + jnp.concatenate(
            [adapter_term, jnp.zeros((own_rows * lax.axis_size("col"), kv_cols), jnp.float32)],
            axis=1,
        ),
        "col",
        scatter_dimension=0,
        tiled=True,
    )
    query_rows = summed[:, :query_cols].astype(jnp.bfloat16)
    kv_cache = summed[:, query_cols:].astype(jnp.bfloat16)
    attend, initial = make_attend(query_rows, segment, first_row, kv_group, head_size, kv_half)
    running_max, running_sum, running_out = attend(
        initial, lax.all_gather(kv_cache, "col", axis=0, tiled=True), jnp.int32(0)
    )
    attention = (running_out / running_sum[:, :, None]).astype(jnp.bfloat16)
    attention = jnp.transpose(attention, (1, 0, 2)).reshape(own_rows, query_cols)
    return (attention, kv_cache)


def solution(mesh):
    return jax.shard_map(
        body,
        mesh=mesh,
        in_specs=(
            P(("dp", "row"), "col"),
            P("col", "row"),
            P("col", None),
            P("dp", "col", None),
            P("dp", None, "row"),
            P(),
            P(),
        ),
        out_specs=(P(("dp", "col"), "row"), P(("dp", "col"), None)),
        check_vma=False,
    )
```

profile of v0, /device:TPU:8, one launch (start us, length us, event | category | flops | bytes accessed | tf_op | source)
XLA Modules:
  0.0 172.5 jit_solution(12041430248315498935)
XLA Ops:
  7.2 0.8 and_select_fusion.5
  8.0 0.7 fusion.40
  8.6 1.3 fusion.46
  10.0 0.2 reduce-window.4
  10.1 0.2 convert_reduce_fusion.1
  11.0 0.1 and_reduce_fusion
  11.2 0.2 fusion.28
  11.4 0.6 copy.29
  11.9 3.2 %all-to-all-start = ((bf16[2,1,4]{2,1,0:T(2,128)(2,1)}), bf16[2,1,4]{2,1,0:T(2,128)(2,1)S(1)}, u32[]{:S(2)}, u32[]{:S(2)}) async-start(bf16[2,1,4]{2,1,0:T(2,128)(2,1)} %copy.29), calls=%async_computation | async-start | bytes 2048 | tf_op jit(solution)/shard_map/all_to_all | solution.py:123
  15.1 0.7 fusion.47
  15.8 0.7 fusion.48
  16.5 0.1 convert_reduce_fusion
  16.6 0.6 broadcast_compare_fusion.8
  17.2 0.1 compare_select_fusion.2
  17.3 0.1 reshape.394
  17.4 18.1 %all_gather.6 = bf16[1024,384]{1,0:T(8,128)(2,1)S(1)} all-gather(bf16[256,384]{1,0:T(8,128)(2,1)} %param.7), channel_id=1, replica_groups=mesh['row'=4,'col'=4,'dp'=2] {'row'}, dimensions={0}, use_global_device_ids=true | all-gather | bytes 983040 | tf_op jit(solution)/shard_map/all_gather | solution.py:75
  35.5 0.1 iota_compare_fusion.2
  35.6 0.6 compare_reduce_fusion
  36.2 4.0 %gather_fusion = bf16[1280,384]{1,0:T(8,128)(2,1)S(1)} fusion(bf16[1024,384]{1,0:T(8,128)(2,1)S(1)} %all_gather.6, s32[2048]{0:T(1024)S(1)} %pad_clamp_fusion), kind=kCustom, calls=%fused_computation | custom fusion | bytes 1971200 | tf_op jit(solution)/shard_map/gather | solution.py:116
  40.2 1.2 broadcast_select_fusion
  41.4 3.6 %all-to-all-start.1 = ((bf16[2,4,160,384]{3,2,1,0:T(8,128)(2,1)}), bf16[2,4,160,384]{3,2,1,0:T(8,128)(2,1)S(1)}, u32[]{:S(2)}, u32[]{:S(2)}) async-start(bf16[2,4,160,384]{3,2,1,0:T(8,128)(2,1)} %broadcast_select_fusion), calls=%async_computation.1 | async-start | bytes 1966080 | tf_op jit(solution)/shard_map/all_to_all | solution.py:122
  45.0 4.3 %select_select_fusion.2 = s32[1024,1]{0,1:T(1,128)S(1)} fusion(s32[]{:T(128)} %bitcast.20, s32[]{:T(128)} %bitcast.21, s32[]{:T(128)} %bitcast.22, s32[]{:T(128)} %bitcast.23, s32[]{:T(128)} %bitcast.24, s32[]{:T(128)} %bitcast.26, s32[]{:T(128)} %bitcast.25, s32[1024,1]{0,1:T(1,128)S(1)} %bitcast.121), kind=kLoop, calls=%fused_computation.53 | loop fusion | flops 15360 | bytes 8220 | tf_op jit(solution)/shard_map/gather | solution.py:131
  49.3 0.1 broadcast_compare_fusion
  49.4 7.1 %all-to-all-done.1 = bf16[2,4,160,384]{3,2,1,0:T(8,128)(2,1)S(1)} async-done(((bf16[2,4,160,384]{3,2,1,0:T(8,128)(2,1)}), bf16[2,4,160,384]{3,2,1,0:T(8,128)(2,1)S(1)}, u32[]{:S(2)}, u32[]{:S(2)}) %all-to-all-start.1) | async-done | bytes 983072 | tf_op jit(solution)/shard_map/all_to_all | solution.py:122
  56.6 1.6 fusion.50
  58.1 5.6 %fusion = f32[2,4,160,384]{3,2,1,0:T(8,128)} fusion(bf16[1024,384,1,1]{1,0,3,2:T(8,128)(2,1)S(1)} %bitcast.117, f32[2,4,160,1024]{3,2,1,0:T(8,128)S(1)} %fusion.50, pred[2,4,1024]{2,1,0:T(4,128)(4,1)S(1)} %broadcast_compare_fusion), kind=kOutput, calls=%fused_computation.2 | convolution fusion | flops 6041108480 | bytes 8003584 | tf_op jit(solution)/shard_map/nkla,af->nklf/dot_general | solution.py:129
  63.7 3.7 %all-to-all-start.2 = ((f32[2,4,160,384]{3,2,1,0:T(8,128)}), f32[2,4,160,384]{3,2,1,0:T(8,128)S(1)}, u32[]{:S(2)}, u32[]{:S(2)}) async-start(f32[2,4,160,384]{3,2,1,0:T(8,128)} %fusion), calls=%async_computation.2 | async-start | bytes 3932160 | tf_op jit(solution)/shard_map/all_to_all | solution.py:130
  67.5 0.7 fusion.49
  68.2 8.7 %select_select_fusion = (s32[1024,1]{0,1:T(1,128)S(1)}, s32[1024,1]{0,1:T(1,128)S(1)}) fusion(s32[]{:T(128)} %bitcast.39, s32[]{:T(128)} %bitcast.40, s32[]{:T(128)} %bitcast.41, s32[]{:T(128)} %bitcast.42, s32[]{:T(128)} %bitcast.43, s32[]{:T(128)} %bitcast.45, s32[]{:T(128)} %bitcast.44, s32[1024,1]{0,1:T(1,128)S(1)} %bitcast.122, s32[]{:T(128)} %bitcast.35, ...), kind=kLoop, calls=%fused_computation.51 | loop fusion | flops 21504 | bytes 12344 | tf_op jit(solution)/shard_map/gather | solution.py:132
  76.9 2.5 %broadcast_select_fusion.2 = (s32[1024]{0:T(1024)S(1)}, s32[1024]{0:T(1024)S(1)}) fusion(pred[1024]{0:T(1024)(128)(4,1)} %compare_reduce_fusion, s32[1024]{0:T(1024)S(1)} %bitcast.125, s32[]{:T(128)} %bitcast.38, s32[1024]{0:T(1024)S(1)} %bitcast.126, s32[]{:T(128)} %bitcast.28, s32[1024]{0:T(1024)S(1)} %bitcast.124, s32[]{:T(128)} %bitcast.19), kind=kLoop, calls=%fused_computation.69 | loop fusion | flops 6144 | bytes 21516 | tf_op jit(solution)/shard_map/gather | solution.py:132
  79.4 9.2 %all-to-all-done.2 = f32[2,4,160,384]{3,2,1,0:T(8,128)S(1)} async-done(((f32[2,4,160,384]{3,2,1,0:T(8,128)}), f32[2,4,160,384]{3,2,1,0:T(8,128)S(1)}, u32[]{:S(2)}, u32[]{:S(2)}) %all-to-all-start.2) | async-done | bytes 1966112 | tf_op jit(solution)/shard_map/all_to_all | solution.py:130
  88.6 4.8 %gather_fusion.1 = f32[1024,384]{1,0:T(8,128)} fusion(f32[1280,384]{1,0:T(8,128)S(1)} %bitcast.115, s32[1024]{0:T(1024)S(1)} %broadcast_clamp_fusion), kind=kCustom, calls=%fused_computation.1 | custom fusion | bytes 3149824 | tf_op jit(solution)/shard_map/gather | solution.py:134
  93.4 1.9 %copy.31 = f32[1024,384]{0,1:T(8,128)S(1)} copy(f32[1024,384]{1,0:T(8,128)} %gather_fusion.1) | data formatting | bytes 3145728 | tf_op jit(solution)/shard_map/gather | solution.py:134
  95.3 0.1 broadcast_select_fusion.1
  95.4 0.8 copy-done.3
  96.3 3.0 %bitcast_add_fusion = f32[1024,896]{0,1:T(8,128)} fusion(f32[1024,384]{0,1:T(8,128)S(1)} %broadcast_select_fusion.1, bf16[1024,384]{1,0:T(8,128)(2,1)S(1)} %all_gather.6, bf16[384,512]{1,0:T(8,128)(2,1)S(1)} %copy-done.2, bf16[384,384]{1,0:T(8,128)(2,1)S(1)} %copy-done.3), kind=kOutput, calls=%fused_computation.4 | convolution fusion | flops 706936832 | bytes 6717440 | tf_op jit(solution)/shard_map/dot_general | solution.py:137
  99.2 0.2 all-gather.2.cloned.1.call-start
  99.5 41.9 %reduce-scatter.2.cloned.1.call-done = f32[256,896]{0,1:T(8,128)} async-done(((f32[1024,896]{0,1:T(8,128)}), f32[256,896]{0,1:T(8,128)}) %reduce-scatter.2.cloned.1.call-update) | async-done | bytes 917520 | tf_op jit(solution)/shard_map/reduce_scatter | solution.py:138
  141.4 1.2 convert.5
  142.6 0.7 slice.41
  143.4 0.1 dynamic_slice.16
  143.5 0.8 fusion.13
  144.3 1.8 %copy.36 = bf16[256,512]{1,0:T(8,128)(2,1)} copy(bf16[256,512]{0,1:T(8,128)(2,1)} %slice.41) | data formatting | bytes 524288
  146.1 14.3 %all-gather.2.cloned.1.call-done = bf16[1024,512]{0,1:T(8,128)(2,1)} async-done(((bf16[256,512]{0,1:T(8,128)(2,1)}), bf16[1024,512]{0,1:T(8,128)(2,1)}) %all-gather.2.cloned.1.call-update) | async-done | bytes 1048592 | tf_op jit(solution)/shard_map/all_gather | solution.py:152
  160.4 1.7 fusion.2
  162.1 0.8 fusion.5
  162.9 1.9 %fusion.17 = bf16[256,3,128]{0,2,1:T(8,128)(2,1)S(1)} fusion(f32[1024,256,3]{1,0,2:T(8,128)S(1)} %get-tuple-element.48, f32[3,256]{1,0:T(4,128)S(1)} %broadcast_maximum_fusion, pred[256,1024]{0,1:T(8,128)(4,1)S(1)} %fusion.13, bf16[1024,512]{0,1:T(8,128)(2,1)} %all-gather.2.cloned.1.call-done, s32[]{:T(128)S(6)} %select_n.133, f32[256,3]{0,1:T(4,128)S(1)} %bitcast.131), kind=kOutput, calls=%fused_computation.18 | convolution fusion | flops 205455360 | bytes 3872772 | tf_op jit(solution)/shard_map/hqk,kd->hqd/dot_general | solution.py:57
  164.9 0.8 copy.35
  (29 shorter events, 0.2 us)
Async XLA Ops:
  7.2 49.4 %copy-start = (bf16[64,384,16]{1,2,0:T(8,128)(2,1)S(1)}, bf16[64,384,16]{1,2,0:T(8,128)(2,1)}, u32[]{:S(2)}) copy-start(bf16[64,384,16]{1,2,0:T(8,128)(2,1)} %param.10) | copy-start | bytes 2359300
  11.9 29.5 %all-to-all-start = ((bf16[2,1,4]{2,1,0:T(2,128)(2,1)}), bf16[2,1,4]{2,1,0:T(2,128)(2,1)S(1)}, u32[]{:S(2)}, u32[]{:S(2)}) async-start(bf16[2,1,4]{2,1,0:T(2,128)(2,1)} %copy.29), calls=%async_computation | async-start | bytes 2048 | tf_op jit(solution)/shard_map/all_to_all | solution.py:123
  41.4 15.2 %all-to-all-start.1 = ((bf16[2,4,160,384]{3,2,1,0:T(8,128)(2,1)}), bf16[2,4,160,384]{3,2,1,0:T(8,128)(2,1)S(1)}, u32[]{:S(2)}, u32[]{:S(2)}) async-start(bf16[2,4,160,384]{3,2,1,0:T(8,128)(2,1)} %broadcast_select_fusion), calls=%async_computation.1 | async-start | bytes 1966080 | tf_op jit(solution)/shard_map/all_to_all | solution.py:122
  56.6 1.6 copy-start.1
  63.7 24.9 %all-to-all-start.2 = ((f32[2,4,160,384]{3,2,1,0:T(8,128)}), f32[2,4,160,384]{3,2,1,0:T(8,128)S(1)}, u32[]{:S(2)}, u32[]{:S(2)}) async-start(f32[2,4,160,384]{3,2,1,0:T(8,128)} %fusion), calls=%async_computation.2 | async-start | bytes 3932160 | tf_op jit(solution)/shard_map/all_to_all | solution.py:130
  67.4 74.0 %reduce-scatter.2.cloned.1.call-start = ((), (), s32[]{:S(2)}) async-start(), calls=%async_computation.4 | async-start | bytes 4587520 | tf_op jit(solution)/shard_map/reduce_scatter | solution.py:138
  93.4 1.9 %copy-start.5 = (pred[1024]{0:T(1024)(128)(4,1)S(1)}, pred[1024]{0:T(1024)(128)(4,1)}, u32[]{:S(2)}) copy-start(pred[1024]{0:T(1024)(128)(4,1)} %get-tuple-element.18) | copy-start | bytes 3076
  93.4 2.1 %copy-start.2 = (bf16[384,512]{1,0:T(8,128)(2,1)S(1)}, bf16[384,512]{1,0:T(8,128)(2,1)}, u32[]{:S(2)}) copy-start(bf16[384,512]{1,0:T(8,128)(2,1)} %param.9) | copy-start | bytes 1179652
  95.3 1.0 copy-start.3
  99.2 44.3 %copy-start.4 = (pred[1024]{0:T(1024)(128)(4,1)S(1)}, pred[1024]{0:T(1024)(128)(4,1)}, u32[]{:S(2)}) copy-start(pred[1024]{0:T(1024)(128)(4,1)} %get-tuple-element.17) | copy-start | bytes 3076
  99.2 61.1 %all-gather.2.cloned.1.call-start = ((), (), s32[]{:S(2)}) async-start(), calls=%async_computation.5 | async-start | bytes 1310720 | tf_op jit(solution)/shard_map/all_gather | solution.py:152
Sparse Core Ops, SparseCore 0:
  99.4 41.9 reduce-scatter.1
  143.5 16.8 all-gather.1
where the time goes:
time: 175 us; the launch traced here: 173 us
  waiting for transfers between devices  72.5 us (41%)
  other arithmetic  24.7 us (14%)
  blocking collectives  18.1 us (10%)
  local copies, waits for them, and re-layouts  17.7 us (10%)
  between operations  14.9 us (9%)
  matrix products  13.7 us (8%)
  starting transfers between devices  10.8 us (6%)
    reduce_scatter x1, waiting for transfers between devices, body(): lax.psum_scatter(partial_value + jnp.concatenate([adapter_term, jnp.zeros...  41.9 us
    all_gather x1, blocking collectives, body(): gathered = lax.all_gather(hidden_states, 'row', axis=0, tiled=True)  18.1 us
    all_gather x1, waiting for transfers between devices, body(): lax.all_gather(kv_cache, 'col', axis=0, tiled=True)  14.3 us
    gather x2, other arithmetic, body(): starts[request_of]  11.2 us
    all_to_all x1, waiting for transfers between devices, body(): lax.all_to_all(adapter_part, 'dp', split_axis=0, concat_axis=0, tiled=True)  9.18 us
    all_to_all x1, waiting for transfers between devices, body(): lax.all_to_all(outgoing, 'dp', split_axis=0, concat_axis=0, tiled=True)  7.14 us
    gather x2, local copies, waits for them, and re-layouts, body(): adapter_term = returned.reshape(-1, query_cols)[flat_index]  6.68 us
    dot_general x1, matrix products, body(): jnp.einsum('nkla,af->nklf', reduced, flat_up, precision=lax.Precision.HIG...  5.56 us
  transfers between devices with their start and end apart: 5, of which 4 were waited for; matrix products, arithmetic and copies ran while one was open for 16% of the time, Pallas kernels for 0%

commit v1 on v0

v1 whole, which is shorter than its diff:
```python
import functools
import math

import jax
import jax.numpy as jnp
from jax import lax
from jax.experimental import pallas as pl
from jax.experimental.pallas import tpu as pltpu
from jax.sharding import PartitionSpec as P

HEAD_DIM = 128
HEADS = 12
KV_HEADS = 2
PREFIX = 64
MESH = pl.DeviceIdType.MESH
FAR = 1 << 20


def remote(src, dst, send_sem, recv_sem, device):
    return pltpu.make_async_remote_copy(
        src_ref=src,
        dst_ref=dst,
        send_sem=send_sem,
        recv_sem=recv_sem,
        device_id=device,
        device_id_type=MESH,
    )


def kernel(
    n_dp,
    h_ref,
    wq_ref,
    wkv_ref,
    dn_ref,
    up_ref,
    len_ref,
    ad_ref,
    att_ref,
    kv_ref,
    hbuf,
    aout,
    ain,
    dsel,
    usel,
    rs_out,
    rs_in,
    keys,
    other,
    a_send,
    a_recv,
    h_send,
    h_recv,
    rs_send,
    rs_recv,
    k_send,
    k_recv,
):
    f32, bf16 = jnp.float32, jnp.bfloat16
    r = lax.axis_index("row")
    c = lax.axis_index("col")
    me = lax.axis_index("dp")
    rows = h_ref.shape[0]
    held, rank = dn_ref.shape[0], dn_ref.shape[1]
    per = ain.shape[1]
    requests = len_ref.shape[1]
    qcols = wq_ref.shape[1]
    block_len = 4 * rows
    back = rows - PREFIX
    sibling = c + 1 - 2 * lax.rem(c, 2)
    across = lax.rem(c + 2, 4)

    barrier = pltpu.get_barrier_semaphore()
    for j in range(1, 4):
        pl.semaphore_signal(
            barrier, inc=1, device_id={"row": lax.rem(r + j, 4)}, device_id_type=MESH
        )
        pl.semaphore_signal(
            barrier, inc=1, device_id={"col": lax.rem(c + j, 4)}, device_id_type=MESH
        )
    for j in range(1, n_dp):
        pl.semaphore_signal(
            barrier, inc=1, device_id={"dp": lax.rem(me + j, n_dp)}, device_id_type=MESH
        )

    def pick(target, store):
        first = me * held
        count = jnp.int32(0)
        picked = [jnp.int32(0)] * per
        for i in range(requests):
            adapter = ad_ref[target, i]
            mine = (adapter >= first) & (adapter < first + held)
            for k in range(per):
                picked[k] = jnp.where(mine & (count == k), adapter - first, picked[k])
            count = count + mine.astype(jnp.int32)
        for k in range(per):
            store(k, dn_ref[picked[k]], up_ref[picked[k]])

    def keep_own(k, down, up):
        ain[me, k, 0] = down
        ain[me, k, 1] = up

    pick(me, keep_own)
    for j in range(1, n_dp):

        def keep_out(k, down, up, j=j):
            aout[j - 1, k, 0] = down
            aout[j - 1, k, 1] = up

        pick(lax.rem(me + j, n_dp), keep_out)
    hbuf[r] = h_ref[...]

    pl.semaphore_wait(barrier, 6 + n_dp - 1)
    copies = []
    for j in range(1, n_dp):
        copies.append(
            remote(
                aout.at[j - 1],
                ain.at[me],
                a_send.at[j - 1],
                a_recv.at[j - 1],
                {"dp": lax.rem(me + j, n_dp)},
            )
        )
    for j in (2, 1, 3):
        copies.append(
            remote(
                h_ref,
                hbuf.at[r],
                h_send.at[j - 1],
                h_recv.at[j - 1],
                {"row": lax.rem(r + j, 4)},
            )
        )
    for copy in copies:
        copy.start()

    total = jnp.int32(0)
    for i in range(requests):
        total = total + len_ref[me, i]
    prefix = block_len - total
    starts, ends = [], []
    run = prefix
    for i in range(requests):
        starts.append(run)
        run = run + len_ref[me, i]
        ends.append(run)
    column = lax.broadcasted_iota(jnp.int32, (1, requests * rank), 1)
    col_start = jnp.zeros((1, requests * rank), jnp.int32)
    col_end = jnp.zeros((1, requests * rank), jnp.int32)
    for i in range(requests):
        here = (column >= i * rank) & (column < (i + 1) * rank)
        col_start = jnp.where(here, starts[i], col_start)
        col_end = jnp.where(here, ends[i], col_end)

    for copy in copies[: n_dp - 1]:
        copy.wait_recv()
    holders = [lax.div(ad_ref[me, i], held) for i in range(requests)]
    for i in range(requests):
        slot = jnp.int32(0)
        for j in range(i):
            slot = slot + (holders[j] == holders[i]).astype(jnp.int32)
        pair = ain[holders[i], jnp.minimum(slot, per - 1)]
        dsel[i * rank : (i + 1) * rank, :] = pair[0]
        usel[i * rank : (i + 1) * rank, :] = pair[1]

    group = lax.div(r * (HEADS // 4), HEADS // KV_HEADS)
    k_col = pl.multiple_of(group * HEAD_DIM, HEAD_DIM)
    v_col = pl.multiple_of((KV_HEADS + group) * HEAD_DIM, HEAD_DIM)
    k_oth = pl.multiple_of((1 - group) * HEAD_DIM, HEAD_DIM)
    v_oth = pl.multiple_of((KV_HEADS + 1 - group) * HEAD_DIM, HEAD_DIM)

    def part(b):
        step = lax.rem(r - b + 4, 4)

        @pl.when(step != 0)
        def _():
            at = lax.rem(step + 3, 4)
            remote(
                h_ref,
                hbuf.at[b],
                h_send.at[at],
                h_recv.at[at],
                {"row": lax.rem(r + 1, 4)},
            ).wait_recv()

        h = hbuf[b]
        low = lax.dot_general(
            h, dsel[...], (((1,), (1,)), ((), ())), preferred_element_type=f32
        )
        pos = b * rows + lax.broadcasted_iota(jnp.int32, (rows, 1), 0)
        low = jnp.where((pos >= col_start) & (pos < col_end), low, 0.0)
        high = low.astype(bf16)
        rest = (low - high.astype(f32)).astype(bf16)
        q = jnp.dot(h, wq_ref[...], preferred_element_type=f32)
        q = q + jnp.dot(high, usel[...], preferred_element_type=f32)
        q = q + jnp.dot(rest, usel[...], preferred_element_type=f32)
        k = jnp.dot(h, wkv_ref[:, pl.ds(k_col, HEAD_DIM)], preferred_element_type=f32)
        v = jnp.dot(h, wkv_ref[:, pl.ds(v_col, HEAD_DIM)], preferred_element_type=f32)
        return q, k, v

    def put(slot, terms):
        q, k, v = terms
        rs_out[slot, :, :qcols] = q.astype(bf16)
        rs_out[slot, :, qcols : qcols + HEAD_DIM] = k.astype(bf16)
        rs_out[slot, :, qcols + HEAD_DIM :] = v.astype(bf16)

    def plus(terms, slot):
        q, k, v = terms
        return (
            q + rs_in[slot, :, :qcols].astype(f32),
            k + rs_in[slot, :, qcols : qcols + HEAD_DIM].astype(f32),
            v + rs_in[slot, :, qcols + HEAD_DIM :].astype(f32),
        )

    def rs_copy(slot, device):
        return remote(
            rs_out.at[slot],
            rs_in.at[slot],
            rs_send.at[slot],
            rs_recv.at[slot],
            {"col": device},
        )

    to_relay = rs_copy(0, sibling)
    to_sibling = rs_copy(1, sibling)
    to_across = rs_copy(2, across)
    put(0, part(3 - c))
    to_relay.start()
    relayed = part(across)
    to_relay.wait_recv()
    put(2, plus(relayed, 0))
    to_across.start()
    put(1, part(sibling))
    to_sibling.start()
    own = part(c)
    to_sibling.wait_recv()
    own = plus(own, 1)
    to_across.wait_recv()
    q, k, v = plus(own, 2)
    q, k, v = q.astype(bf16), k.astype(bf16), v.astype(bf16)

    keys[rows:, :HEAD_DIM] = k
    keys[rows:, HEAD_DIM:] = v
    firsts = [
        remote(
            keys.at[pl.ds(rows, PREFIX)],
            keys.at[pl.ds(0, PREFIX)],
            k_send.at[j - 1],
            k_recv.at[0],
            {"col": lax.rem(c + j, 4)},
        )
        for j in range(1, 4)
    ]
    onward = remote(
        keys.at[pl.ds(rows + PREFIX, back)],
        keys.at[pl.ds(PREFIX, back)],
        k_send.at[3],
        k_recv.at[1],
        {"col": lax.rem(c + 1, 4)},
    )
    swap = remote(
        keys.at[pl.ds(rows, rows)],
        other,
        k_send.at[4],
        k_recv.at[2],
        {"row": lax.rem(r + 2, 4)},
    )

    @pl.when(c < 3)
    def _():
        onward.start()

    @pl.when(c == 0)
    def _():
        for copy in firsts:
            copy.start()
        keys[:rows, :] = jnp.zeros((rows, 2 * HEAD_DIM), bf16)

    swap.start()
    kv_ref[:, pl.ds(k_col, HEAD_DIM)] = k
    kv_ref[:, pl.ds(v_col, HEAD_DIM)] = v

    base = c * rows
    q_pos = base + lax.broadcasted_iota(jnp.int32, (rows, 1), 0)
    seg_start = jnp.zeros((rows, 1), jnp.int32)
    for i in range(requests):
        seg_start = jnp.where(q_pos >= starts[i], starts[i], seg_start)
    at = lax.broadcasted_iota(jnp.int32, (1, 2 * rows), 1)
    k_pos = jnp.where(at < PREFIX, at, base - rows + at)
    k_pos = jnp.where((at < rows) & (c == 0), FAR, k_pos)
    allowed = (k_pos <= q_pos) & ((k_pos >= seg_start) | (k_pos < prefix))

    @pl.when(c > 0)
    def _():
        firsts[0].wait_recv()
        onward.wait_recv()

    key_rows = keys[:, :HEAD_DIM]
    value_rows = keys[:, HEAD_DIM:]
    scale = 1.0 / math.sqrt(HEAD_DIM)
    for n in range(qcols // HEAD_DIM):
        cols = slice(n * HEAD_DIM, (n + 1) * HEAD_DIM)
        score = (
            lax.dot_general(
                q[:, cols], key_rows, (((1,), (1,)), ((), ())), preferred_element_type=f32
            )
            * scale
        )
        score = jnp.where(allowed, score, -1e30)
        weight = jnp.exp(score - jnp.max(score, axis=1, keepdims=True))
        weight = jnp.where(allowed, weight, 0.0)
        row_total = jnp.sum(weight, axis=1, keepdims=True)
        mixed = jnp.dot(weight.astype(bf16), value_rows, preferred_element_type=f32)
        att_ref[:, cols] = (mixed / row_total).astype(bf16)

    swap.wait_recv()
    kv_ref[:, pl.ds(k_oth, HEAD_DIM)] = other[:, :HEAD_DIM]
    kv_ref[:, pl.ds(v_oth, HEAD_DIM)] = other[:, HEAD_DIM:]

    for copy in copies:
        copy.wait_send()
    for copy in (to_relay, to_sibling, to_across, swap):
        copy.wait_send()

    @pl.when(c < 3)
    def _():
        onward.wait_send()

    @pl.when(c == 0)
    def _():
        for copy in firsts:
            copy.wait_send()


def body(hidden, w_query, w_key_value, adapter_down, adapter_up, req_lengths, req_adapter):
    n_dp = lax.axis_size("dp")
    rows, width = hidden.shape
    qcols = w_query.shape[1]
    rank = adapter_down.shape[2]
    requests = req_lengths.shape[1]
    per = (requests + n_dp - 1) // n_dp
    sums = qcols + 2 * HEAD_DIM
    bf16 = jnp.bfloat16
    vmem = pl.BlockSpec(memory_space=pltpu.VMEM)
    smem = pl.BlockSpec(memory_space=pltpu.SMEM)
    dma = pltpu.SemaphoreType.DMA
    return pl.pallas_call(
        functools.partial(kernel, n_dp),
        out_shape=(
            jax.ShapeDtypeStruct((rows, qcols), bf16),
            jax.ShapeDtypeStruct((rows, w_key_value.shape[1]), bf16),
        ),
        in_specs=[vmem] * 5 + [smem] * 2,
        out_specs=(vmem, vmem),
        scratch_shapes=[
            pltpu.VMEM((4, rows, width), bf16),
            pltpu.VMEM((n_dp - 1, per, 2, rank, width), bf16),
            pltpu.VMEM((n_dp, per, 2, rank, width), bf16),
            pltpu.VMEM((requests * rank, width), bf16),
            pltpu.VMEM((requests * rank, qcols), bf16),
            pltpu.VMEM((3, rows, sums), bf16),
            pltpu.VMEM((3, rows, sums), bf16),
            pltpu.VMEM((2 * rows, 2 * HEAD_DIM), bf16),
            pltpu.VMEM((rows, 2 * HEAD_DIM), bf16),
            dma((n_dp - 1,)),
            dma((n_dp - 1,)),
            dma((3,)),
            dma((3,)),
            dma((3,)),
            dma((3,)),
            dma((5,)),
            dma((3,)),
        ],
        compiler_params=pltpu.CompilerParams(
            collective_id=0, has_side_effects=True, vmem_limit_bytes=48 << 20
        ),
    )(
        hidden,
        w_query,
        w_key_value,
        jnp.transpose(adapter_down, (0, 2, 1)),
        adapter_up,
        req_lengths,
        req_adapter,
    )


def solution(mesh):
    return jax.shard_map(
        body,
        mesh=mesh,
        in_specs=(
            P(("dp", "row"), "col"),
            P("col", "row"),
            P("col", None),
            P("dp", "col", None),
            P("dp", None, "row"),
            P(),
            P(),
        ),
        out_specs=(P(("dp", "col"), "row"), P(("dp", "col"), None)),
        check_vma=False,
    )
```

time: 175 us -> 49.2 us (0.28)
  the two profiles are of different devices: /device:TPU:8 before, /device:TPU:0 now
where the time goes in v1:
time: 49.2 us; the launch traced here: 48.9 us
  Pallas kernels  40.3 us (82%)
  local copies, waits for them, and re-layouts  7.88 us (16%)
  between operations  0.66 us (1%)
    pallas_call x1, Pallas kernels, body(): pl.pallas_call(functools.partial(kernel, n_dp), out_shape=(jax.ShapeDtype...  40.3 us
    unnamed x16, local copies, waits for them, and re-layouts  7.88 us

profile of v1, /device:TPU:0, one launch (start us, length us, event | category | flops | bytes accessed | tf_op | source)
XLA Modules:
  0.0 48.9 jit_solution(3699120382775467718)
XLA Ops:
  0.6 0.0 copy-start.5
  0.6 0.7 %copy-done.5 = s32[2,8]{1,0:T(2,128)S(1)} copy-done((s32[2,8]{1,0:T(2,128)S(1)}, s32[2,8]{1,0:T(2,128)}, u32[]{:S(2)}) %copy-start.5) | copy-done | bytes 88
  1.3 0.0 copy-start
  1.3 1.1 %copy-done = bf16[64,384,16]{1,2,0:T(8,128)(2,1)S(1)} copy-done((bf16[64,384,16]{1,2,0:T(8,128)(2,1)S(1)}, bf16[64,384,16]{1,2,0:T(8,128)(2,1)}, u32[]{:S(2)}) %copy-start) | copy-done | bytes 786456
  2.4 0.0 copy-start.1
  2.4 1.1 %copy-done.1 = bf16[64,16,384]{2,1,0:T(8,128)(2,1)S(1)} copy-done((bf16[64,16,384]{2,1,0:T(8,128)(2,1)S(1)}, bf16[64,16,384]{2,1,0:T(8,128)(2,1)}, u32[]{:S(2)}) %copy-start.1) | copy-done | bytes 786456
  3.6 0.0 copy-start.2
  3.6 1.0 %copy-done.2 = bf16[384,512]{1,0:T(8,128)(2,1)S(1)} copy-done((bf16[384,512]{1,0:T(8,128)(2,1)S(1)}, bf16[384,512]{1,0:T(8,128)(2,1)}, u32[]{:S(2)}) %copy-start.2) | copy-done | bytes 393240
  4.6 0.0 copy-start.3
  4.6 1.0 %copy-done.3 = bf16[384,384]{1,0:T(8,128)(2,1)S(1)} copy-done((bf16[384,384]{1,0:T(8,128)(2,1)S(1)}, bf16[384,384]{1,0:T(8,128)(2,1)}, u32[]{:S(2)}) %copy-start.3) | copy-done | bytes 294936
  5.5 0.0 copy-start.4
  5.5 0.9 %copy-done.4 = bf16[256,384]{1,0:T(8,128)(2,1)S(1)} copy-done((bf16[256,384]{1,0:T(8,128)(2,1)S(1)}, bf16[256,384]{1,0:T(8,128)(2,1)}, u32[]{:S(2)}) %copy-start.4) | copy-done | bytes 196632
  6.5 0.0 copy-start.6
  6.5 0.7 %copy-done.6 = s32[2,8]{1,0:T(2,128)S(1)} copy-done((s32[2,8]{1,0:T(2,128)S(1)}, s32[2,8]{1,0:T(2,128)}, u32[]{:S(2)}) %copy-start.6) | copy-done | bytes 88
  7.1 40.3 %shard_map.86 = (bf16[256,384]{1,0:T(8,128)(2,1)S(1)}, bf16[256,512]{1,0:T(8,128)(2,1)S(1)}) custom-call(bf16[256,384]{1,0:T(8,128)(2,1)S(1)} %copy-done.4, bf16[384,384]{1,0:T(8,128)(2,1)S(1)} %copy-done.3, bf16[384,512]{1,0:T(8,128)(2,1)S(1)} %copy-done.2, bf16[64,16,384]{2,1,0:T(8,128)(2,1)S(1)} %bitcast.1, bf16[64,16,384]{2,1,0:T(8,128)(2,1)S(1)} %copy-done.1, ...), custom_call_target="tpu_custom_call" | custom-call | tf_op jit(solution)/shard_map/pallas_call | solution.py:348
  47.5 0.7 %copy.11 = bf16[256,384]{1,0:T(8,128)(2,1)} copy(bf16[256,384]{1,0:T(8,128)(2,1)S(1)} %get-tuple-element.4) | data formatting | bytes 393216
  48.2 0.7 %copy.12 = bf16[256,512]{1,0:T(8,128)(2,1)} copy(bf16[256,512]{1,0:T(8,128)(2,1)S(1)} %get-tuple-element.5) | data formatting | bytes 524288
Async XLA Ops:
  0.6 0.7 %copy-start.5 = (s32[2,8]{1,0:T(2,128)S(1)}, s32[2,8]{1,0:T(2,128)}, u32[]{:S(2)}) copy-start(s32[2,8]{1,0:T(2,128)} %len_ref.1) | copy-start | bytes 196
  1.3 1.1 %copy-start = (bf16[64,384,16]{1,2,0:T(8,128)(2,1)S(1)}, bf16[64,384,16]{1,2,0:T(8,128)(2,1)}, u32[]{:S(2)}) copy-start(bf16[64,384,16]{1,2,0:T(8,128)(2,1)} %param.10) | copy-start | bytes 2359300
  2.4 1.1 %copy-start.1 = (bf16[64,16,384]{2,1,0:T(8,128)(2,1)S(1)}, bf16[64,16,384]{2,1,0:T(8,128)(2,1)}, u32[]{:S(2)}) copy-start(bf16[64,16,384]{2,1,0:T(8,128)(2,1)} %up_ref.1) | copy-start | bytes 2359300
  3.6 1.0 %copy-start.2 = (bf16[384,512]{1,0:T(8,128)(2,1)S(1)}, bf16[384,512]{1,0:T(8,128)(2,1)}, u32[]{:S(2)}) copy-start(bf16[384,512]{1,0:T(8,128)(2,1)} %wkv_ref.1) | copy-start | bytes 1179652
  4.6 1.0 %copy-start.3 = (bf16[384,384]{1,0:T(8,128)(2,1)S(1)}, bf16[384,384]{1,0:T(8,128)(2,1)}, u32[]{:S(2)}) copy-start(bf16[384,384]{1,0:T(8,128)(2,1)} %wq_ref.1) | copy-start | bytes 884740
  5.5 0.9 %copy-start.4 = (bf16[256,384]{1,0:T(8,128)(2,1)S(1)}, bf16[256,384]{1,0:T(8,128)(2,1)}, u32[]{:S(2)}) copy-start(bf16[256,384]{1,0:T(8,128)(2,1)} %h_ref.1) | copy-start | bytes 589828
  6.5 0.7 %copy-start.6 = (s32[2,8]{1,0:T(2,128)S(1)}, s32[2,8]{1,0:T(2,128)}, u32[]{:S(2)}) copy-start(s32[2,8]{1,0:T(2,128)} %ad_ref.1) | copy-start | bytes 196

commit v2 on v1

--- a/solution.py
+++ b/solution.py
@@ -29,15 +29,22 @@
 
 def kernel(
     n_dp,
-    h_ref,
+    h_hbm,
+    wq_hbm,
+    wkv_hbm,
+    dn_hbm,
+    up_hbm,
+    len_hbm,
+    ad_hbm,
+    att_ref,
+    kv_ref,
     wq_ref,
     wkv_ref,
     dn_ref,
     up_ref,
     len_ref,
     ad_ref,
-    att_ref,
-    kv_ref,
+    loads,
     hbuf,
     aout,
     ain,
@@ -47,6 +54,7 @@
     rs_in,
     keys,
     other,
+    mine_sum,
     a_send,
     a_recv,
     h_send,
@@ -60,7 +68,7 @@
     r = lax.axis_index("row")
     c = lax.axis_index("col")
     me = lax.axis_index("dp")
-    rows = h_ref.shape[0]
+    rows = h_hbm.shape[0]
     held, rank = dn_ref.shape[0], dn_ref.shape[1]
     per = ain.shape[1]
     requests = len_ref.shape[1]
@@ -69,6 +77,27 @@
     back = rows - PREFIX
     sibling = c + 1 - 2 * lax.rem(c, 2)
     across = lax.rem(c + 2, 4)
+    group = lax.div(r * (HEADS // 4), HEADS // KV_HEADS)
+    k_col = pl.multiple_of(group * HEAD_DIM, HEAD_DIM)
+    v_col = pl.multiple_of((KV_HEADS + group) * HEAD_DIM, HEAD_DIM)
+    k_oth = pl.multiple_of((1 - group) * HEAD_DIM, HEAD_DIM)
+    v_oth = pl.multiple_of((KV_HEADS + 1 - group) * HEAD_DIM, HEAD_DIM)
+
+    def load(n, src, dst):
+        copy = pltpu.make_async_copy(src, dst, loads.at[n])
+        copy.start()
+        return copy
+
+    get_ad = load(0, ad_hbm, ad_ref)
+    get_h = load(1, h_hbm, hbuf.at[r])
+    get_dn = load(2, dn_hbm, dn_ref)
+    get_up = load(3, up_hbm, up_ref)
+    get_len = load(4, len_hbm, len_ref)
+    get_wq = load(5, wq_hbm, wq_ref)
+    get_k = load(6, wkv_hbm.at[:, pl.ds(k_col, HEAD_DIM)], wkv_ref.at[:, pl.ds(0, HEAD_DIM)])
+    get_v = load(
+        7, wkv_hbm.at[:, pl.ds(v_col, HEAD_DIM)], wkv_ref.at[:, pl.ds(HEAD_DIM, HEAD_DIM)]
+    )
 
     barrier = pltpu.get_barrier_semaphore()
     for j in range(1, 4):
@@ -100,7 +129,9 @@
         ain[me, k, 0] = down
         ain[me, k, 1] = up
 
-    pick(me, keep_own)
+    get_ad.wait()
+    get_dn.wait()
+    get_up.wait()
     for j in range(1, n_dp):
 
         def keep_out(k, down, up, j=j):
@@ -108,9 +139,23 @@
             aout[j - 1, k, 1] = up
 
         pick(lax.rem(me + j, n_dp), keep_out)
-    hbuf[r] = h_ref[...]
+    get_h.wait()
+
+    def pass_on(b, sem, up_row):
+        return remote(
+            hbuf.at[b], hbuf.at[b], h_send.at[sem], h_recv.at[b], {"row": lax.rem(r + up_row, 4)}
+        )
 
     pl.semaphore_wait(barrier, 6 + n_dp - 1)
+
+    @pl.when(r < 3)
+    def _():
+        pass_on(r, 4, 1).start()
+
+    @pl.when(r > 0)
+    def _():
+        pass_on(r, 5, 3).start()
+
     copies = []
     for j in range(1, n_dp):
         copies.append(
@@ -122,18 +167,10 @@
                 {"dp": lax.rem(me + j, n_dp)},
             )
         )
-    for j in (2, 1, 3):
-        copies.append(
-            remote(
-                h_ref,
-                hbuf.at[r],
-                h_send.at[j - 1],
-                h_recv.at[j - 1],
-                {"row": lax.rem(r + j, 4)},
-            )
-        )
     for copy in copies:
         copy.start()
+    pick(me, keep_own)
+    get_len.wait()
 
     total = jnp.int32(0)
     for i in range(requests):
@@ -153,7 +190,7 @@
         col_start = jnp.where(here, starts[i], col_start)
         col_end = jnp.where(here, ends[i], col_end)
 
-    for copy in copies[: n_dp - 1]:
+    for copy in copies:
         copy.wait_recv()
     holders = [lax.div(ad_ref[me, i], held) for i in range(requests)]
     for i in range(requests):
@@ -164,25 +201,22 @@
         dsel[i * rank : (i + 1) * rank, :] = pair[0]
         usel[i * rank : (i + 1) * rank, :] = pair[1]
 
-    group = lax.div(r * (HEADS // 4), HEADS // KV_HEADS)
-    k_col = pl.multiple_of(group * HEAD_DIM, HEAD_DIM)
-    v_col = pl.multiple_of((KV_HEADS + group) * HEAD_DIM, HEAD_DIM)
-    k_oth = pl.multiple_of((1 - group) * HEAD_DIM, HEAD_DIM)
-    v_oth = pl.multiple_of((KV_HEADS + 1 - group) * HEAD_DIM, HEAD_DIM)
+    get_wq.wait()
+    get_k.wait()
+    get_v.wait()
 
     def part(b):
-        step = lax.rem(r - b + 4, 4)
-
-        @pl.when(step != 0)
-        def _():
-            at = lax.rem(step + 3, 4)
-            remote(
-                h_ref,
-                hbuf.at[b],
-                h_send.at[at],
-                h_recv.at[at],
-                {"row": lax.rem(r + 1, 4)},
-            ).wait_recv()
+        @pl.when(b != r)
+        def _():
+            pass_on(b, b, 1).wait_recv()
+
+        @pl.when((b < r) & (r < 3))
+        def _():
+            pass_on(b, b, 1).start()
+
+        @pl.when((b > r) & (r > 0))
+        def _():
+            pass_on(b, b, 3).start()
 
         h = hbuf[b]
         low = lax.dot_general(
@@ -195,22 +229,16 @@
         q = jnp.dot(h, wq_ref[...], preferred_element_type=f32)
         q = q + jnp.dot(high, usel[...], preferred_element_type=f32)
         q = q + jnp.dot(rest, usel[...], preferred_element_type=f32)
-        k = jnp.dot(h, wkv_ref[:, pl.ds(k_col, HEAD_DIM)], preferred_element_type=f32)
-        v = jnp.dot(h, wkv_ref[:, pl.ds(v_col, HEAD_DIM)], preferred_element_type=f32)
-        return q, k, v
+        return q, jnp.dot(h, wkv_ref[...], preferred_element_type=f32)
 
     def put(slot, terms):
-        q, k, v = terms
-        rs_out[slot, :, :qcols] = q.astype(bf16)
-        rs_out[slot, :, qcols : qcols + HEAD_DIM] = k.astype(bf16)
-        rs_out[slot, :, qcols + HEAD_DIM :] = v.astype(bf16)
+        rs_out[slot, :, :qcols] = terms[0].astype(bf16)
+        rs_out[slot, :, qcols:] = terms[1].astype(bf16)
 
     def plus(terms, slot):
-        q, k, v = terms
         return (
-            q + rs_in[slot, :, :qcols].astype(f32),
-            k + rs_in[slot, :, qcols : qcols + HEAD_DIM].astype(f32),
-            v + rs_in[slot, :, qcols + HEAD_DIM :].astype(f32),
+            terms[0] + rs_in[slot, :, :qcols].astype(f32),
+            terms[1] + rs_in[slot, :, qcols:].astype(f32),
         )
 
     def rs_copy(slot, device):
@@ -222,26 +250,38 @@
             {"col": device},
         )
 
-    to_relay = rs_copy(0, sibling)
-    to_sibling = rs_copy(1, sibling)
-    to_across = rs_copy(2, across)
-    put(0, part(3 - c))
-    to_relay.start()
-    relayed = part(across)
-    to_relay.wait_recv()
-    put(2, plus(relayed, 0))
-    to_across.start()
-    put(1, part(sibling))
-    to_sibling.start()
-    own = part(c)
-    to_sibling.wait_recv()
-    own = plus(own, 1)
-    to_across.wait_recv()
-    q, k, v = plus(own, 2)
-    q, k, v = q.astype(bf16), k.astype(bf16), v.astype(bf16)
-
-    keys[rows:, :HEAD_DIM] = k
-    keys[rows:, HEAD_DIM:] = v
+    half = lax.div(r, 2)
+    inner = r + half * (3 - 2 * r)
+    for step in range(4):
+        b = step + inner * (1 - 2 * step) if step < 2 else step + 0 * r
+        b = b + half * (3 - 2 * b)
+        odd = lax.rem(c + b, 2)
+        far = lax.rem(lax.div(c, 2) + lax.div(b, 2), 2)
+        terms = part(b)
+
+        @pl.when(odd == 1)
+        def _():
+            put(1 - far, terms)
+            rs_copy(1 - far, sibling).start()
+
+        @pl.when((odd == 0) & (far == 1))
+        def _():
+            rs_copy(0, sibling).wait_recv()
+            put(2, plus(terms, 0))
+            rs_copy(2, across).start()
+
+        @pl.when(c == b)
+        def _():
+            mine_sum[:, :qcols] = terms[0]
+            mine_sum[:, qcols:] = terms[1]
+
+    rs_copy(1, sibling).wait_recv()
+    own = plus((mine_sum[:, :qcols], mine_sum[:, qcols:]), 1)
+    rs_copy(2, across).wait_recv()
+    q, kv = plus(own, 2)
+    q, kv = q.astype(bf16), kv.astype(bf16)
+
+    keys[rows:, :] = kv
     firsts = [
         remote(
             keys.at[pl.ds(rows, PREFIX)],
@@ -278,8 +318,8 @@
         keys[:rows, :] = jnp.zeros((rows, 2 * HEAD_DIM), bf16)
 
     swap.start()
-    kv_ref[:, pl.ds(k_col, HEAD_DIM)] = k
-    kv_ref[:, pl.ds(v_col, HEAD_DIM)] = v
+    kv_ref[:, pl.ds(k_col, HEAD_DIM)] = kv[:, :HEAD_DIM]
+    kv_ref[:, pl.ds(v_col, HEAD_DIM)] = kv[:, HEAD_DIM:]
 
     base = c * rows
     q_pos = base + lax.broadcasted_iota(jnp.int32, (rows, 1), 0)
@@ -320,8 +360,22 @@
 
     for copy in copies:
         copy.wait_send()
-    for copy in (to_relay, to_sibling, to_across, swap):
+    for copy in (rs_copy(0, sibling), rs_copy(1, sibling), rs_copy(2, across), swap):
         copy.wait_send()
+
+    @pl.when(r < 3)
+    def _():
+        pass_on(r, 4, 1).wait_send()
+
+    @pl.when(r > 0)
+    def _():
+        pass_on(r, 5, 3).wait_send()
+
+    for b in range(4):
+
+        @pl.when(((b < r) & (r < 3)) | ((b > r) & (r > 0)))
+        def _():
+            pass_on(b, b, 1).wait_send()
 
     @pl.when(c < 3)
     def _():
@@ -343,7 +397,6 @@
     sums = qcols + 2 * HEAD_DIM
     bf16 = jnp.bfloat16
     vmem = pl.BlockSpec(memory_space=pltpu.VMEM)
-    smem = pl.BlockSpec(memory_space=pltpu.SMEM)
     dma = pltpu.SemaphoreType.DMA
     return pl.pallas_call(
         functools.partial(kernel, n_dp),
@@ -351,9 +404,16 @@
             jax.ShapeDtypeStruct((rows, qcols), bf16),
             jax.ShapeDtypeStruct((rows, w_key_value.shape[1]), bf16),
         ),
-        in_specs=[vmem] * 5 + [smem] * 2,
+        in_specs=[pl.BlockSpec(memory_space=pltpu.HBM)] * 7,
         out_specs=(vmem, vmem),
         scratch_shapes=[
+            pltpu.VMEM(w_query.shape, bf16),
+            pltpu.VMEM((width, 2 * HEAD_DIM), bf16),
+            pltpu.VMEM((adapter_down.shape[0], rank, width), bf16),
+            pltpu.VMEM(adapter_up.shape, bf16),
+            pltpu.SMEM(req_lengths.shape, jnp.int32),
+            pltpu.SMEM(req_adapter.shape, jnp.int32),
+            dma((8,)),
             pltpu.VMEM((4, rows, width), bf16),
             pltpu.VMEM((n_dp - 1, per, 2, rank, width), bf16),
             pltpu.VMEM((n_dp, per, 2, rank, width), bf16),
@@ -363,17 +423,18 @@
             pltpu.VMEM((3, rows, sums), bf16),
             pltpu.VMEM((2 * rows, 2 * HEAD_DIM), bf16),
             pltpu.VMEM((rows, 2 * HEAD_DIM), bf16),
+            pltpu.VMEM((rows, sums), jnp.float32),
             dma((n_dp - 1,)),
             dma((n_dp - 1,)),
-            dma((3,)),
-            dma((3,)),
+            dma((6,)),
+            dma((4,)),
             dma((3,)),
             dma((3,)),
             dma((5,)),
             dma((3,)),
         ],
         compiler_params=pltpu.CompilerParams(
-            collective_id=0, has_side_effects=True, vmem_limit_bytes=48 << 20
+            collective_id=0, has_side_effects=True, vmem_limit_bytes=60 << 20
         ),
     )(
         hidden,

time: 49.2 us -> 39.3 us (0.80)
  the two profiles are of different devices: /device:TPU:0 before, /device:TPU:8 now
where the time goes in v2:
time: 39.3 us; the launch traced here: 39.1 us
  Pallas kernels  36.1 us (92%)
  local copies, waits for them, and re-layouts  2.37 us (6%)
  between operations  0.65 us (2%)
    pallas_call x1, Pallas kernels, body(): pl.pallas_call(functools.partial(kernel, n_dp), out_shape=(jax.ShapeDtype...  36.1 us
    unnamed x4, local copies, waits for them, and re-layouts  2.37 us

profile of v2, /device:TPU:8, one launch (start us, length us, event | category | flops | bytes accessed | tf_op | source)
XLA Modules:
  0.0 39.1 jit_solution(9896108058416623136)
XLA Ops:
  0.6 36.1 %shard_map.86 = (bf16[256,384]{1,0:T(8,128)(2,1)}, bf16[256,512]{1,0:T(8,128)(2,1)}) custom-call(bf16[256,384]{1,0:T(8,128)(2,1)} %h_hbm.1, bf16[384,384]{1,0:T(8,128)(2,1)} %wq_hbm.1, bf16[384,512]{1,0:T(8,128)(2,1)} %wkv_hbm.1, bf16[64,16,384]{2,1,0:T(8,128)(2,1)} %bitcast.1, bf16[64,16,384]{2,1,0:T(8,128)(2,1)} %up_hbm.1, s32[2,8]{1,0:T(2,128)} %len_hbm.1, ...), custom_call_target="tpu_custom_call" | custom-call | tf_op jit(solution)/shard_map/pallas_call | solution.py:401
  36.8 0.0 copy-start
  36.8 1.7 %copy.11 = bf16[256,384]{1,0:T(8,128)(2,1)} copy(bf16[256,384]{1,0:T(8,128)(2,1)} %get-tuple-element.4) | data formatting | bytes 393216
  38.4 0.0 copy-done
  38.4 0.7 %copy.12 = bf16[256,512]{1,0:T(8,128)(2,1)} copy(bf16[256,512]{1,0:T(8,128)(2,1)S(1)} %copy-done) | data formatting | bytes 524288
Async XLA Ops:
  36.8 1.7 %copy-start = (bf16[256,512]{1,0:T(8,128)(2,1)S(1)}, bf16[256,512]{1,0:T(8,128)(2,1)}, u32[]{:S(2)}) copy-start(bf16[256,512]{1,0:T(8,128)(2,1)} %get-tuple-element.5) | copy-start | bytes 786436

commit v3 on v2

--- a/solution.py
+++ b/solution.py
@@ -190,6 +190,31 @@
         col_start = jnp.where(here, starts[i], col_start)
         col_end = jnp.where(here, ends[i], col_end)
 
+    def take(b):
+        @pl.when(b != r)
+        def _():
+            pass_on(b, b, 1).wait_recv()
+
+        @pl.when((b < r) & (r < 3))
+        def _():
+            pass_on(b, b, 1).start()
+
+        @pl.when((b > r) & (r > 0))
+        def _():
+            pass_on(b, b, 3).start()
+
+    half = lax.div(r, 2)
+    inner = r + half * (3 - 2 * r)
+    order = []
+    for step in range(4):
+        b = step + inner * (1 - 2 * step) if step < 2 else step + 0 * r
+        order.append(b + half * (3 - 2 * b))
+
+    @pl.when(inner == 1)
+    def _():
+        take(order[1])
+        take(order[2])
+
     for copy in copies:
         copy.wait_recv()
     holders = [lax.div(ad_ref[me, i], held) for i in range(requests)]
@@ -206,18 +231,6 @@
     get_v.wait()
 
     def part(b):
-        @pl.when(b != r)
-        def _():
-            pass_on(b, b, 1).wait_recv()
-
-        @pl.when((b < r) & (r < 3))
-        def _():
-            pass_on(b, b, 1).start()
-
-        @pl.when((b > r) & (r > 0))
-        def _():
-            pass_on(b, b, 3).start()
-
         h = hbuf[b]
         low = lax.dot_general(
             h, dsel[...], (((1,), (1,)), ((), ())), preferred_element_type=f32
@@ -250,11 +263,15 @@
             {"col": device},
         )
 
-    half = lax.div(r, 2)
-    inner = r + half * (3 - 2 * r)
-    for step in range(4):
-        b = step + inner * (1 - 2 * step) if step < 2 else step + 0 * r
-        b = b + half * (3 - 2 * b)
+    for step, b in enumerate(order):
+        if step in (1, 2):
+
+            @pl.when(inner == 0)
+            def _():
+                take(b)
+
+        elif step == 3:
+            take(b)
         odd = lax.rem(c + b, 2)
         far = lax.rem(lax.div(c, 2) + lax.div(b, 2), 2)
         terms = part(b)

time: 39.3 us -> 34.5 us (0.88)
  Pallas kernels: 36.1 us -> 31.3 us
    pallas_call x1, Pallas kernels: 36.1 us -> 31.3 us  [body(): pl.pallas_call(functools.partial(kernel, n_dp), out_shape=(jax.ShapeDtype...]
where the time goes in v3:
time: 34.5 us; the launch traced here: 34.3 us
  Pallas kernels  31.3 us (91%)
  local copies, waits for them, and re-layouts  2.37 us (7%)
  between operations  0.65 us (2%)
    pallas_call x1, Pallas kernels, body(): pl.pallas_call(functools.partial(kernel, n_dp), out_shape=(jax.ShapeDtype...  31.3 us
    unnamed x4, local copies, waits for them, and re-layouts  2.37 us

profile of v3, /device:TPU:8, one launch (start us, length us, event | category | flops | bytes accessed | tf_op | source)
XLA Modules:
  0.0 34.3 jit_solution(8214448626869738735)
XLA Ops:
  0.6 31.3 %shard_map.86 = (bf16[256,384]{1,0:T(8,128)(2,1)}, bf16[256,512]{1,0:T(8,128)(2,1)}) custom-call(bf16[256,384]{1,0:T(8,128)(2,1)} %h_hbm.1, bf16[384,384]{1,0:T(8,128)(2,1)} %wq_hbm.1, bf16[384,512]{1,0:T(8,128)(2,1)} %wkv_hbm.1, bf16[64,16,384]{2,1,0:T(8,128)(2,1)} %bitcast.1, bf16[64,16,384]{2,1,0:T(8,128)(2,1)} %up_hbm.1, s32[2,8]{1,0:T(2,128)} %len_hbm.1, ...), custom_call_target="tpu_custom_call" | custom-call | tf_op jit(solution)/shard_map/pallas_call | solution.py:418
  31.9 0.0 copy-start
  31.9 1.7 %copy.11 = bf16[256,384]{1,0:T(8,128)(2,1)} copy(bf16[256,384]{1,0:T(8,128)(2,1)} %get-tuple-element.4) | data formatting | bytes 393216
  33.6 0.0 copy-done
  33.6 0.7 %copy.12 = bf16[256,512]{1,0:T(8,128)(2,1)} copy(bf16[256,512]{1,0:T(8,128)(2,1)S(1)} %copy-done) | data formatting | bytes 524288
Async XLA Ops:
  31.9 1.7 %copy-start = (bf16[256,512]{1,0:T(8,128)(2,1)S(1)}, bf16[256,512]{1,0:T(8,128)(2,1)}, u32[]{:S(2)}) copy-start(bf16[256,512]{1,0:T(8,128)(2,1)} %get-tuple-element.5) | copy-start | bytes 786436
